TPU v7x, 32 devices: a whole 2x2x4 slice. The times are simulated.
32 devices in a mesh: grp: 2 (over y), ao: 4 (over z), pb: 2 (over x), rep: 2 (over core).
Axes of the slice: x: 2, y: 2, z: 4, core: 2. Of those that a mesh axis runs over, the one named last changes fastest.
Arguments:
- g_occ: bfloat16 [8, 3, 64, 64], P(('grp', 'ao')), parts along dimension 0, may hold values from -0.4375 to 0.4375
- g_vir: bfloat16 [8, 3, 64, 64], P(('grp', 'ao')), parts along dimension 0, may hold values from -0.4375 to 0.4375
- three_q: bfloat16 [4, 3, 128, 4096], P('ao', None, ('pb', 'rep')), may hold values from -6 to 6
- three_centre_p: bfloat16 [4, 64, 64, 4096], P('ao', ('grp', 'pb', 'rep')), parts along dimension 1, may hold values from -0.046875 to 0.046875
- slot_ids: int32 [4, 64], P('ao', ('grp', 'pb', 'rep')), parts along dimension 1, may hold values from 0 to 24, as said below
Outputs:
- chi: float32 [2048, 128], P(('grp', 'pb'), ('ao', 'rep')), parts along dimension 0
There are 2 independent parts, one for each index of `grp`. A program takes and returns all parts, laid end to end along the dimension named above; an argument that names none is the same for every part. Nothing has to cross between parts.
Inputs may be any that keep to these rules, and one draw needn't show every extreme that they name: slot_ids[a, j] is a block code: a value below 24 names aux block (its value) // 3 among the 8 aux blocks of the slot's pb index and the nu offset (its value) % 3; the value 3 * 8 marks an empty slot whose three_centre_p entries are not used. The live codes among the 16 slots of one AO block and one pb index are distinct. Every pb index has an AO block whose slots on every device are all live.
All inputs are finite; a program needn't handle non-finite values.
Results may differ from a plain program's by a relative error of at most 0.0041.
Values may be sent and summed in bfloat16 or wider, within the bound.
A program may use at most 64 MiB of HBM per device.

v0:
```python
import jax
import jax.numpy as jnp
from jax import lax
from jax.sharding import PartitionSpec as P


def with_halo(block, sides, width):
    for axis, dim in sides:
        count = lax.axis_size(axis)
        forward = [(i, i + 1) for i in range(count - 1)]
        forward.append((count - 1, 0))
        backward = [(target, source) for source, target in forward]
        low = lax.ppermute(
            lax.slice_in_dim(block, block.shape[dim] - width, None, axis=dim), axis, forward
        )
        high = lax.ppermute(lax.slice_in_dim(block, 0, width, axis=dim), axis, backward)
        block = jnp.concatenate([low, block, high], axis=dim)
    return block


def per_device(g_occ, g_vir, three_q, three_centre_p, slot_ids):
    q_rows = three_q.shape[2]
    block_size = g_occ.shape[2]
    flat_size = block_size * block_size
    vir_flat = g_vir.reshape(1, 3, 1, flat_size)
    joined = jnp.concatenate((three_q, vir_flat), axis=2)
    extended_rows = with_halo(joined, (("ao", 0),), 1)
    occ_rows = g_occ[0]
    w_parts = []
    for n in range(3):
        w_total = jnp.zeros((q_rows, block_size, block_size), jnp.float32)
        for d in range(3):
            u_inner = jnp.zeros((q_rows * block_size, block_size), jnp.float32)
            for s in range(3):
                t = d + s - n
                if 0 <= t <= 2:
                    left_part = extended_rows[d, s, :q_rows].reshape(
                        q_rows * block_size, block_size
                    )
                    right_part = extended_rows[n, t, q_rows].reshape(block_size, block_size)
                    u_inner = u_inner + lax.dot_general(
                        left_part,
                        right_part,
                        (((1,), (1,)), ((), ())),
                        preferred_element_type=jnp.float32,
                    )
            rounded = u_inner.astype(jnp.bfloat16).reshape(q_rows, block_size, block_size)
            w_total = w_total + jnp.einsum(
                "ik,qkj->qij", occ_rows[d], rounded, preferred_element_type=jnp.float32
            )
        w_parts.append(w_total.astype(jnp.bfloat16).reshape(q_rows, flat_size))
    w_local = jnp.stack(w_parts, axis=0)
    slot_codes = slot_ids[0]
    slot_data = three_centre_p[0]
    slot_count = slot_data.shape[0]
    code_limit = 3 * slot_count
    is_live = (slot_codes < code_limit).astype(jnp.float32)
    p_index = jnp.minimum(slot_codes // 3, slot_count - 1)
    o_index = slot_codes % 3
    total_q = q_rows * lax.axis_size("pb") * lax.axis_size("rep")
    initial = jnp.zeros((slot_count, block_size, total_q), jnp.float32)
    zero_index = jnp.zeros((), jnp.int32)
    running = initial
    shard_piece = lax.all_gather(w_local, ("pb", "rep"), axis=1, tiled=True)
    width_rows = shard_piece.shape[1]
    start_col = jnp.asarray(jnp.int32(0))
    for c in range(slot_count):
        chosen = lax.dynamic_index_in_dim(shard_piece, o_index[c], 0, keepdims=False)
        product = lax.dot_general(
            slot_data[c], chosen, (((1,), (1,)), ((), ())), preferred_element_type=jnp.float32
        )
        product = product * is_live[c]
        current = lax.dynamic_slice(
            running, (p_index[c], zero_index, start_col), (1, block_size, width_rows)
        )
        running = lax.dynamic_update_slice(
            running, current + product[None], (p_index[c], zero_index, start_col)
        )
    partial_chi = running.reshape(slot_count * block_size, total_q)
    return lax.psum_scatter(partial_chi, ("ao", "rep"), scatter_dimension=1, tiled=True)


def solution(mesh):
    placed = (
        P(("grp", "ao"), None, None, None),
        P(("grp", "ao"), None, None, None),
        P("ao", None, ("pb", "rep"), None),
        P("ao", ("grp", "pb", "rep"), None, None),
        P("ao", ("grp", "pb", "rep")),
    )
    return jax.shard_map(
        per_device,
        mesh=mesh,
        in_specs=placed,
        out_specs=P(("grp", "pb"), ("ao", "rep")),
        check_vma=False,
    )
```

profile of v0, /device:TPU:0, one launch (start us, length us, event | category | flops | bytes accessed | tf_op | source)
XLA Modules:
  0.0 190.9 jit_solution(1499873610309805481)
XLA Ops:
  7.4 2.1 %constant_dynamic-update-slice_fusion = bf16[1,3,33,4096]{3,2,1,0:T(8,128)(2,1)} fusion(bf16[1,3,32,4096]{3,2,1,0:T(8,128)(2,1)} %param.7), kind=kLoop, calls=%fused_computation.137 | loop fusion | bytes 1572864
  10.2 5.0 %collective-permute-start.1 = (bf16[1,3,33,4096]{3,2,1,0:T(8,128)(2,1)}, bf16[1,3,33,4096]{3,2,1,0:T(8,128)(2,1)S(1)}, u32[]{:S(2)}, u32[]{:S(2)}) collective-permute-start(bf16[1,3,33,4096]{3,2,1,0:T(8,128)(2,1)} %copy_dynamic-update-slice_fusion), channel_id=1, source_target_pairs={{4,0},{8,4},{12,8},{0,12},{5,1},{9,5},{13,9},{1,13},{6,2},{10,6},{... | collective-permute-start | bytes 2433032 | tf_op jit(solution)/shard_map/ppermute | solution.py:16
  19.9 17.9 %collective-permute-done.1 = bf16[1,3,33,4096]{3,2,1,0:T(8,128)(2,1)S(1)} collective-permute-done((bf16[1,3,33,4096]{3,2,1,0:T(8,128)(2,1)}, bf16[1,3,33,4096]{3,2,1,0:T(8,128)(2,1)S(1)}, u32[]{:S(2)}, u32[]{:S(2)}) %collective-permute-start.1) | collective-permute-done | bytes 811040 | tf_op jit(solution)/shard_map/ppermute | solution.py:16
  41.9 16.7 %collective-permute-done = bf16[1,3,33,4096]{3,2,1,0:T(8,128)(2,1)} collective-permute-done((bf16[1,3,33,4096]{3,2,1,0:T(8,128)(2,1)}, bf16[1,3,33,4096]{3,2,1,0:T(8,128)(2,1)}, u32[]{:S(2)}, u32[]{:S(2)}) %collective-permute-start) | collective-permute-done | bytes 811040 | tf_op jit(solution)/shard_map/ppermute | solution.py:13
  60.8 1.9 %fusion.112 = (bf16[1,1,32,4096]{3,2,1,0:T(8,128)(2,1)}, bf16[1,1,32,4096]{3,2,1,0:T(8,128)(2,1)S(1)}, bf16[1,1,32,4096]{3,2,1,0:T(8,128)(2,1)}) fusion(bf16[1,3,33,4096]{3,2,1,0:T(8,128)(2,1)} %collective-permute-done), kind=kLoop, calls=%fused_computation.151 | loop fusion | bytes 1572864 | tf_op jit(solution)/shard_map/slice | solution.py:37
  65.1 2.0 %fusion.9 = bf16[2048,64]{0,1:T(8,128)(2,1)} fusion(f32[64,2048]{1,0:T(8,128)} %fusion.124, bf16[64,64]{1,0:T(8,128)(2,1)S(1)} %reshape_squeeze.88, bf16[2048,64]{1,0:T(8,128)(2,1)S(1)} %reshape_squeeze.81), kind=kOutput, calls=%fused_computation.19 | convolution fusion | flops 17039360 | bytes 1056768 | tf_op jit(solution)/shard_map/dot_general | solution.py:41
  67.2 1.5 reshape_squeeze.82
  68.6 1.5 reshape.89
  71.1 2.1 %fusion.6 = bf16[2048,64]{0,1:T(8,128)(2,1)} fusion(f32[2048,64]{0,1:T(8,128)} %fusion.123, bf16[2048,64]{1,0:T(8,128)(2,1)S(1)} %reshape_squeeze.82, bf16[64,64]{1,0:T(8,128)(2,1)S(1)} %reshape_squeeze.84), kind=kOutput, calls=%fused_computation.14 | convolution fusion | flops 17039360 | bytes 1056768 | tf_op jit(solution)/shard_map/dot_general | solution.py:41
  73.2 2.3 %reshape.87 = bf16[32,64,64]{1,0,2:T(8,128)(2,1)} reshape(bf16[2048,64]{0,1:T(8,128)(2,1)} %fusion.6) | data formatting | bytes 524288 | tf_op jit(solution)/shard_map/reshape | solution.py:47
  75.4 2.3 %reshape_squeeze.90 = bf16[2048,64]{1,0:T(8,128)(2,1)} reshape(bf16[1,1,32,4096]{3,2,1,0:T(8,128)(2,1)} %get-tuple-element.18) | data formatting | bytes 524288 | tf_op jit(solution)/shard_map/reshape;squeeze | solution.py:37
  80.0 2.3 %reshape.90 = bf16[32,64,64]{1,0,2:T(8,128)(2,1)} reshape(bf16[2048,64]{0,1:T(8,128)(2,1)} %fusion.8) | data formatting | bytes 524288 | tf_op jit(solution)/shard_map/reshape | solution.py:47
  84.3 2.3 %reshape.84 = bf16[32,64,64]{1,0,2:T(8,128)(2,1)} reshape(bf16[2048,64]{0,1:T(8,128)(2,1)} %convolution_convert_fusion.1) | data formatting | bytes 524288 | tf_op jit(solution)/shard_map/reshape | solution.py:47
  86.6 2.3 %reshape_squeeze.36 = bf16[2048,64]{1,0:T(8,128)(2,1)} reshape(bf16[1,1,32,4096]{3,2,1,0:T(8,128)(2,1)} %get-tuple-element.14) | data formatting | bytes 524288 | tf_op jit(solution)/shard_map/reshape;squeeze | solution.py:37
  89.4 1.5 reshape_squeeze.76
  134.9 2.8 %fusion.39 = f32[8,64,128]{2,1,0:T(8,128)S(1)} fusion(f32[8,64,128]{2,1,0:T(8,128)S(1)} %broadcast_in_dim.27, s32[]{:T(128)S(6)} %select_n.71, bf16[3,128,4096]{2,1,0:T(8,128)(2,1)} %all-gather.2.cloned.1.call-done, s32[]{:T(128)S(6)} %select_n.69, bf16[1,8,64,4096]{3,2,1,0:T(8,128)(2,1)} %param.8, f32[]{:T(128)} %bitcast.18), kind=kOutput, calls=%fused_computation.63 | convolution fusion | flops 67117056 | bytes 1606152 | tf_op jit(solution)/shard_map/dot_general | solution.py:69
  137.6 2.5 %fusion.37 = f32[8,64,128]{2,1,0:T(8,128)S(1)} fusion(f32[8,64,128]{2,1,0:T(8,128)S(1)} %fusion.39, s32[]{:T(128)S(6)} %select_n.72, bf16[3,128,4096]{2,1,0:T(8,128)(2,1)} %all-gather.2.cloned.1.call-done, s32[]{:T(128)S(6)} %select_n.73, bf16[1,8,64,4096]{3,2,1,0:T(8,128)(2,1)} %param.8, f32[]{:T(128)} %bitcast.28), kind=kOutput, calls=%fused_computation.60 | convolution fusion | flops 67125248 | bytes 1638920 | tf_op jit(solution)/shard_map/dot_general | solution.py:69
  140.1 2.4 %fusion.34 = f32[8,64,128]{2,1,0:T(8,128)S(1)} fusion(f32[8,64,128]{2,1,0:T(8,128)S(1)} %fusion.37, s32[]{:T(128)S(6)} %select_n.74, bf16[3,128,4096]{2,1,0:T(8,128)(2,1)} %all-gather.2.cloned.1.call-done, s32[]{:T(128)S(6)} %select_n.75, bf16[1,8,64,4096]{3,2,1,0:T(8,128)(2,1)} %param.8, f32[]{:T(128)} %bitcast.35), kind=kOutput, calls=%fused_computation.56 | convolution fusion | flops 67125248 | bytes 1638920 | tf_op jit(solution)/shard_map/dot_general | solution.py:69
  142.5 2.1 %fusion.31 = f32[8,64,128]{2,1,0:T(8,128)S(1)} fusion(f32[8,64,128]{2,1,0:T(8,128)S(1)} %fusion.34, s32[]{:T(128)S(6)} %select_n.76, bf16[3,128,4096]{2,1,0:T(8,128)(2,1)S(1)} %copy-done, s32[]{:T(128)S(6)} %select_n.77, bf16[1,8,64,4096]{3,2,1,0:T(8,128)(2,1)} %param.8, f32[]{:T(128)} %bitcast.42), kind=kOutput, calls=%fused_computation.52 | convolution fusion | flops 67125248 | bytes 1638920 | tf_op jit(solution)/shard_map/dot_general | solution.py:69
  144.6 2.2 %fusion.28 = f32[8,64,128]{2,1,0:T(8,128)S(1)} fusion(f32[8,64,128]{2,1,0:T(8,128)S(1)} %fusion.31, s32[]{:T(128)S(6)} %select_n.78, bf16[3,128,4096]{2,1,0:T(8,128)(2,1)S(1)} %copy-done, s32[]{:T(128)S(6)} %select_n.79, bf16[1,8,64,4096]{3,2,1,0:T(8,128)(2,1)} %param.8, f32[]{:T(128)} %bitcast.49), kind=kOutput, calls=%fused_computation.48 | convolution fusion | flops 67125248 | bytes 1638920 | tf_op jit(solution)/shard_map/dot_general | solution.py:69
  146.8 2.1 %fusion.25 = f32[8,64,128]{2,1,0:T(8,128)S(1)} fusion(f32[8,64,128]{2,1,0:T(8,128)S(1)} %fusion.28, s32[]{:T(128)S(6)} %select_n.80, bf16[3,128,4096]{2,1,0:T(8,128)(2,1)S(1)} %copy-done, s32[]{:T(128)S(6)} %select_n.81, bf16[1,8,64,4096]{3,2,1,0:T(8,128)(2,1)} %param.8, f32[]{:T(128)} %bitcast.56), kind=kOutput, calls=%fused_computation.44 | convolution fusion | flops 67125248 | bytes 1638920 | tf_op jit(solution)/shard_map/dot_general | solution.py:69
  148.9 2.2 %fusion.22 = f32[8,64,128]{2,1,0:T(8,128)S(1)} fusion(f32[8,64,128]{2,1,0:T(8,128)S(1)} %fusion.25, s32[]{:T(128)S(6)} %select_n.82, bf16[3,128,4096]{2,1,0:T(8,128)(2,1)S(1)} %copy-done, s32[]{:T(128)S(6)} %select_n.83, bf16[1,8,64,4096]{3,2,1,0:T(8,128)(2,1)} %param.8, f32[]{:T(128)} %bitcast.63), kind=kOutput, calls=%fused_computation.40 | convolution fusion | flops 67125248 | bytes 1638920 | tf_op jit(solution)/shard_map/dot_general | solution.py:69
  151.1 2.2 %fusion.19 = f32[8,64,128]{2,1,0:T(8,128)S(1)} fusion(f32[8,64,128]{2,1,0:T(8,128)S(1)} %fusion.22, s32[]{:T(128)S(6)} %select_n.84, bf16[3,128,4096]{2,1,0:T(8,128)(2,1)S(1)} %copy-done, s32[]{:T(128)S(6)} %select_n.85, bf16[1,8,64,4096]{3,2,1,0:T(8,128)(2,1)} %param.8, f32[]{:T(128)} %bitcast.70), kind=kOutput, calls=%fused_computation.36 | convolution fusion | flops 67125248 | bytes 1638920 | tf_op jit(solution)/shard_map/dot_general | solution.py:69
  154.1 29.9 %reduce-scatter.2.cloned.1.call-done = f32[512,16]{0,1:T(8,128)} async-done(((f32[512,128]{0,1:T(8,128)}), f32[512,16]{0,1:T(8,128)}) %reduce-scatter.2.cloned.1.call-update) | async-done | bytes 32784 | tf_op jit(solution)/shard_map/reduce_scatter | solution.py:80
  (83 shorter events, 35.2 us)
Async XLA Ops:
  6.5 128.3 %all-gather.2.cloned.1.call-start = ((), (), s32[]{:S(2)}) async-start(), calls=%async_computation.1 | async-start | bytes 3932160 | tf_op jit(solution)/shard_map/all_gather | solution.py:64
  10.2 27.5 %collective-permute-start.1 = (bf16[1,3,33,4096]{3,2,1,0:T(8,128)(2,1)}, bf16[1,3,33,4096]{3,2,1,0:T(8,128)(2,1)S(1)}, u32[]{:S(2)}, u32[]{:S(2)}) collective-permute-start(bf16[1,3,33,4096]{3,2,1,0:T(8,128)(2,1)} %copy_dynamic-update-slice_fusion), channel_id=1, source_target_pairs={{4,0},{8,4},{12,8},{0,12},{5,1},{9,5},{13,9},{1,13},{6,2},{10,6},{... | collective-permute-start | bytes 2433032 | tf_op jit(solution)/shard_map/ppermute | solution.py:16
  15.2 43.3 %collective-permute-start = (bf16[1,3,33,4096]{3,2,1,0:T(8,128)(2,1)}, bf16[1,3,33,4096]{3,2,1,0:T(8,128)(2,1)}, u32[]{:S(2)}, u32[]{:S(2)}) collective-permute-start(bf16[1,3,33,4096]{3,2,1,0:T(8,128)(2,1)} %copy_dynamic-update-slice_fusion), channel_id=1, source_target_pairs={{0,4},{4,8},{8,12},{12,0},{1,5},{5,9},{9,13},{13,1},{2,6},{6,10},{... | collective-permute-start | bytes 2433032 | tf_op jit(solution)/shard_map/ppermute | solution.py:13
  86.6 8.3 %copy-start.4 = (bf16[1,3,64,64]{3,2,1,0:T(8,128)(2,1)S(1)}, bf16[1,3,64,64]{3,2,1,0:T(8,128)(2,1)}, u32[]{:S(2)}) copy-start(bf16[1,3,64,64]{3,2,1,0:T(8,128)(2,1)} %param.5) | copy-start | bytes 73732
  94.9 1.0 copy-start.2
  96.0 3.5 %copy-start.3 = (bf16[32,64,64]{1,0,2:T(8,128)(2,1)S(1)}, bf16[32,64,64]{1,0,2:T(8,128)(2,1)}, u32[]{:S(2)}) copy-start(bf16[32,64,64]{1,0,2:T(8,128)(2,1)} %reshape.84) | copy-start | bytes 786436
  99.5 1.7 copy-start.1
  100.9 2.4 %copy-start.5 = (s32[1,8]{1,0:T(1,128)S(1)}, s32[1,8]{1,0:T(1,128)}, u32[]{:S(2)}) copy-start(s32[1,8]{1,0:T(1,128)} %param.9) | copy-start | bytes 100
  103.2 80.8 %reduce-scatter.2.cloned.1.call-start = ((), (), s32[]{:S(2)}) async-start(), calls=%async_computation.2 | async-start | bytes 294912 | tf_op jit(solution)/shard_map/reduce_scatter | solution.py:80
  134.8 7.6 %copy-start = (bf16[3,128,4096]{2,1,0:T(8,128)(2,1)S(1)}, bf16[3,128,4096]{2,1,0:T(8,128)(2,1)}, u32[]{:S(2)}) copy-start(bf16[3,128,4096]{2,1,0:T(8,128)(2,1)} %all-gather.2.cloned.1.call-done) | copy-start | bytes 9437188
Sparse Core Ops, SparseCore 0:
  103.4 27.9 all-gather.1
  154.2 29.7 reduce-scatter.1
where the time goes:
time: 193 us; the launch traced here: 191 us
  waiting for transfers between devices  64.5 us (33%)
  between operations  43.9 us (23%)
  matrix products  40 us (21%)
  local copies, waits for them, and re-layouts  36.4 us (19%)
  starting transfers between devices  5.1 us (3%)
    reduce_scatter x1, waiting for transfers between devices, per_device(): lax.psum_scatter(partial_chi, ('ao', 'rep'), scatter_dimension=1, tiled=T...  29.9 us
    dot_general x8, matrix products, per_device(): lax.dot_general(slot_data[c], chosen, (((1,), (1,)), ((), ())), preferred...  18.3 us
    dot_general x19, matrix products, per_device(): lax.dot_general(left_part, right_part, (((1,), (1,)), ((), ())), preferre...  17.9 us
    ppermute x1, waiting for transfers between devices, with_halo(): lax.ppermute(lax.slice_in_dim(block, 0, width, axis=dim), axis, backward)  17.9 us
    ppermute x1, waiting for transfers between devices, with_halo(): lax.ppermute(lax.slice_in_dim(block, block.shape[dim] - width, None, axis...  16.7 us
    reshape x9, local copies, waits for them, and re-layouts, per_device(): u_inner.astype(jnp.bfloat16).reshape(q_rows, block_size, block_size)  10.9 us
    another operation x9, local copies, waits for them, and re-layouts, per_device(): extended_rows[d, s, :q_rows].reshape(q_rows * block_size, block_size)  10.2 us
    ppermute x1, starting transfers between devices, with_halo(): lax.ppermute(lax.slice_in_dim(block, 0, width, axis=dim), axis, backward)  5.05 us
  transfers between devices with their start and end apart: 4, of which 3 were waited for; matrix products, arithmetic and copies ran while one was open for 5% of the time, Pallas kernels for 0%

commit v1 on v0

v1 whole, which is shorter than its diff:
```python
import functools

import jax
import jax.numpy as jnp
from jax import lax
from jax.experimental import pallas as pl
from jax.experimental.pallas import tpu as pltpu
from jax.sharding import PartitionSpec as P

MESH = pl.DeviceIdType.MESH
BF = jnp.bfloat16
F32 = jnp.float32
CHUNK_Q = 4
PASS_CHUNKS = 2


def kernel(n_ao, n_pb, chunks, inv, tq, gv_in, go_in, p_in, out,
           tlo, thi, gv, go, bmat, glu, pbuf, xs, wsend, wbuf, wf, wt, chi, rs,
           s_t, r_tlo, r_thi, s_gv, r_gv, s_go, r_go, s_p, r_p, l_sem,
           s_w, r_w, s_rs, r_rs):
    g, a = lax.axis_index("grp"), lax.axis_index("ao")
    p, r = lax.axis_index("pb"), lax.axis_index("rep")
    up, down = lax.rem(a + 1, n_ao), lax.rem(a + n_ao - 1, n_ao)
    other = 1 - g

    def at_p(step):
        return lax.rem(p + step, n_pb)

    def from_p(step):
        return lax.rem(p + n_pb - step, n_pb)

    barrier = pltpu.get_barrier_semaphore()
    peers = [(g, lax.rem(a + i, n_ao), p, j) for i in range(1, n_ao) for j in (0, 1)]
    peers += [(g, a, p, 1 - r)]
    peers += [(other, row, p, r) for row in (down, a, up)]
    peers += [(grp, a, at_p(i), r) for i in range(1, n_pb) for grp in (g, other)]
    for peer in peers:
        pl.semaphore_signal(barrier, inc=1, device_id=peer, device_id_type=MESH)
    pl.semaphore_wait(barrier, len(peers))

    def remote(src, dst, send, recv, peer):
        return pltpu.make_async_remote_copy(
            src_ref=src, dst_ref=dst, send_sem=send, recv_sem=recv,
            device_id=peer, device_id_type=MESH)

    sends = []

    def post(*args):
        copy = remote(*args)
        copy.start()
        sends.append(copy)

    post(go_in, go.at[1], s_go.at[0], r_go.at[0], (other, a, p, r))
    count = 0
    for dg, grp in ((0, g), (1, other)):
        for n, row in ((0, up), (1, a), (2, down)):
            if dg == 0 and n == 1:
                continue
            post(gv_in, gv.at[dg, n], s_gv.at[count], r_gv.at[dg * 3 + n], (grp, row, p, r))
            count += 1
    for c in range(chunks):
        rows = pl.ds(c * CHUNK_Q, CHUNK_Q)
        post(tq.at[rows], tlo.at[rows], s_t.at[2 * c], r_tlo.at[c], (g, up, p, r))
        post(tq.at[rows], thi.at[rows], s_t.at[2 * c + 1], r_thi.at[c], (g, down, p, r))
    half = p_in.shape[0]
    mine = pl.ds(r * half, half)
    post(p_in, pbuf.at[mine], s_p.at[0], r_p.at[0], (g, a, p, 1 - r))
    own_p = pltpu.make_async_copy(p_in, pbuf.at[mine], l_sem.at[0])
    own_p.start()
    pbuf[2 * half] = jnp.zeros(pbuf.shape[1:], BF)

    def landed(dst, sem):
        remote(dst, dst, s_go.at[0], sem, (other, a, p, r)).wait_recv()

    go[0] = go_in[...]
    gv[0, 1] = gv_in[...]
    landed(go.at[1], r_go.at[0])
    lane = lax.broadcasted_iota(jnp.int32, (128, 128), 1)
    for dg in range(2):
        whole = go[dg]
        for u in range(5):
            low, high = 32 * max(0, u - 2), 32 * (min(2, u) + 1)
            glu[u, dg * 128:(dg + 1) * 128, :] = jnp.where(
                (lane >= low) & (lane < high), whole, jnp.zeros_like(whole))
    lane = lax.broadcasted_iota(jnp.int32, (64, 128), 1)
    for dg in range(2):
        for n in range(3):
            if not (dg == 0 and n == 1):
                landed(gv.at[dg, n], r_gv.at[dg * 3 + n])
            for t in range(3):
                both = gv[dg, n, t]
                left = jnp.where(lane < 64, both, jnp.zeros_like(both))
                right = jnp.where(lane < 64, jnp.zeros_like(both), both)
                k = (dg * 3 + n) * 3 + t
                bmat[k, 0:64] = left
                bmat[k, 64:128] = left
                bmat[k, 128:192] = right
                bmat[k, 192:256] = right

    pair_lane = lax.rem(lax.broadcasted_iota(jnp.int32, (64, 256), 1), 128) < 64
    sources = [(dg, dp) for dg in range(2) for dp in range(n_pb)]
    rows_w = CHUNK_Q * 32

    def make_w(c):
        rows = pl.ds(c * CHUNK_Q, CHUNK_Q)
        landed(tlo.at[rows], r_tlo.at[c])
        landed(thi.at[rows], r_thi.at[c])
        for q0 in range(0, CHUNK_Q, 2):
            for u in range(5):
                cols = []
                for q in (c * CHUNK_Q + q0, c * CHUNK_Q + q0 + 1):
                    parts = [ref[q, min(max(u - d, 0), 2)]
                             for d, ref in enumerate((tlo, tq, thi))]
                    cols.append(jnp.concatenate(parts, axis=0))
                right = jnp.concatenate(cols, axis=1)
                both = jnp.dot(glu[u][:, :96], right, preferred_element_type=F32)
                for dg in range(2):
                    base = dg * 128
                    x = jnp.where(pair_lane, both[base:base + 64], both[base + 64:base + 128])
                    x = x.astype(BF)
                    for i in range(2):
                        at = (q0 + i) * 32
                        xs[dg, u, at:at + 32, 0:128] = x[0:32, i * 128:(i + 1) * 128]
                        xs[dg, u, at:at + 32, 128:256] = x[32:64, i * 128:(i + 1) * 128]
        for dg in (1, 0):
            for n in range(3):
                total = jnp.zeros((rows_w, 128), F32)
                for t in range(3):
                    total = total + jnp.dot(
                        xs[dg, n + t], bmat[(dg * 3 + n) * 3 + t], preferred_element_type=F32)
                wsend[c, dg, n] = total.astype(BF)
            grp = g if dg == 0 else other
            for dp in range(n_pb):
                if dg == 0 and dp == 0:
                    continue
                k = c * len(sources) + dg * n_pb + dp
                post(wsend.at[c, dg], wbuf.at[c, dg * n_pb + dp], s_w.at[k], r_w.at[k],
                     (grp, a, at_p(dp), r))

    def contract(first):
        for c in range(first, first + PASS_CHUNKS):
            for k in range(len(sources)):
                if k > 0:
                    landed(wbuf.at[c, k], r_w.at[c * len(sources) + k])
                for n in range(3):
                    block = wsend[c, 0, n] if k == 0 else wbuf[c, k, n]
                    at = (k * PASS_CHUNKS + c - first) * rows_w
                    wf[n, at:at + rows_w] = block.astype(F32)
        count_q = len(sources) * PASS_CHUNKS * CHUNK_Q
        for n in range(3):
            for tile in range(32):
                wt[n, :, tile * 128:(tile + 1) * 128] = wf[
                    n, pl.ds(tile, count_q, stride=32), :].astype(BF)
        for group in range(2):
            total = jnp.zeros((count_q, 256), F32)
            for n in range(3):
                blocks = []
                for i in range(4):
                    blocks.append(pbuf[inv[(group * 4 + i) * 3 + n]])
                total = total + lax.dot_general(
                    wt[n], jnp.concatenate(blocks, axis=0), (((1,), (1,)), ((), ())),
                    preferred_element_type=F32)
            for k in range(len(sources)):
                width = PASS_CHUNKS * CHUNK_Q
                chi[k, first * CHUNK_Q:first * CHUNK_Q + width, group * 256:(group + 1) * 256] = (
                    total[k * width:(k + 1) * width])

    for c in range(chunks):
        make_w(c)
        if c == PASS_CHUNKS:
            own_p.wait()
            theirs = pl.ds((1 - r) * half, half)
            landed(pbuf.at[theirs], r_p.at[0])
            contract(0)
    contract(PASS_CHUNKS)

    later = []
    for k, (dg, dp) in enumerate(sources):
        row = from_p(dp) * 2 + r
        rep = g if dg == 0 else other
        slot = lax.rem(a - row + n_ao, n_ao)
        same = (row == a) & (rep == r)
        far = remote(chi.at[k], rs.at[slot], s_rs.at[k], r_rs.at[slot], (g, row, p, rep))
        near = pltpu.make_async_copy(chi.at[k], rs.at[slot], r_rs.at[slot])

        @pl.when(same)
        def _():
            near.start()

        @pl.when(jnp.logical_not(same))
        def _():
            far.start()

        later.append((same, far))
    total = None
    for slot in range(n_ao):
        landed(rs.at[slot], r_rs.at[slot])
        total = rs[slot] if total is None else total + rs[slot]
    out[...] = total
    for same, far in later:
        @pl.when(jnp.logical_not(same))
        def _():
            far.wait_send()
    for copy in sends:
        copy.wait_send()


def per_device(n_ao, n_pb, g_occ, g_vir, three_q, three_centre_p, slot_ids):
    q_half = three_q.shape[2] // 2
    chunks = q_half // CHUNK_Q
    g = lax.axis_index("grp")
    tq = lax.dynamic_slice_in_dim(three_q[0], g * q_half, q_half, axis=1)
    tq = tq.reshape(3, q_half, 32, 128).transpose(1, 0, 2, 3)
    gv = g_vir[0].transpose(0, 2, 1)
    gv = jnp.concatenate((gv, gv), axis=2)
    go = g_occ[0].reshape(3, 32, 2, 32, 2).transpose(4, 2, 1, 0, 3).reshape(128, 96)
    go = jnp.pad(go, ((0, 0), (0, 32)))
    slots = slot_ids.shape[1]
    codes = lax.all_gather(slot_ids[0], "rep", tiled=True)
    hit = codes[None, :] == jnp.arange(3 * slots, dtype=jnp.int32)[:, None]
    numbers = jnp.arange(2 * slots, dtype=jnp.int32)
    inv = jnp.min(jnp.where(hit, numbers[None, :], 2 * slots), axis=1)
    p_flat = three_centre_p[0]
    n_src = 2 * n_pb
    count_q = n_src * PASS_CHUNKS * CHUNK_Q
    dma = pltpu.SemaphoreType.DMA
    vmem = pl.BlockSpec(memory_space=pltpu.VMEM)
    out = pl.pallas_call(
        functools.partial(kernel, n_ao, n_pb, chunks),
        out_shape=jax.ShapeDtypeStruct((q_half, slots * 64), F32),
        in_specs=[pl.BlockSpec(memory_space=pltpu.SMEM), vmem, vmem, vmem,
                  pl.BlockSpec(memory_space=pl.ANY)],
        out_specs=vmem,
        scratch_shapes=[
            pltpu.VMEM((q_half, 3, 32, 128), BF),
            pltpu.VMEM((q_half, 3, 32, 128), BF),
            pltpu.VMEM((2, 3, 3, 64, 128), BF),
            pltpu.VMEM((2, 128, 128), BF),
            pltpu.VMEM((18, 256, 128), BF),
            pltpu.VMEM((5, 256, 128), BF),
            pltpu.VMEM((2 * slots + 1, 64, 4096), BF),
            pltpu.VMEM((2, 5, CHUNK_Q * 32, 256), BF),
            pltpu.VMEM((chunks, 2, 3, CHUNK_Q * 32, 128), BF),
            pltpu.VMEM((chunks, n_src, 3, CHUNK_Q * 32, 128), BF),
            pltpu.VMEM((3, count_q * 32, 128), F32),
            pltpu.VMEM((3, count_q, 4096), BF),
            pltpu.VMEM((n_src, q_half, slots * 64), F32),
            pltpu.VMEM((n_ao, q_half, slots * 64), F32),
            dma((2 * chunks,)), dma((chunks,)), dma((chunks,)),
            dma((5,)), dma((6,)), dma((1,)), dma((1,)), dma((1,)), dma((1,)), dma((1,)),
            dma((chunks * n_src,)), dma((chunks * n_src,)),
            dma((n_src,)), dma((n_ao,)),
        ],
        compiler_params=pltpu.CompilerParams(
            collective_id=0, has_side_effects=True, vmem_limit_bytes=56 * 1024 * 1024),
    )(inv, tq, gv, go, p_flat)
    return out.T


def solution(mesh):
    placed = (
        P(("grp", "ao"), None, None, None),
        P(("grp", "ao"), None, None, None),
        P("ao", None, ("pb", "rep"), None),
        P("ao", ("grp", "pb", "rep"), None, None),
        P("ao", ("grp", "pb", "rep")),
    )
    return jax.shard_map(
        functools.partial(per_device, mesh.shape["ao"], mesh.shape["pb"]),
        mesh=mesh,
        in_specs=placed,
        out_specs=P(("grp", "pb"), ("ao", "rep")),
        check_vma=False,
    )
```

time: 193 us -> 65.5 us (0.34)
  waiting for transfers between devices: 64.5 us -> 0 us
  Pallas kernels: 0 us -> 48.6 us
  between operations: 43.9 us -> 0.71 us
  matrix products: 40 us -> 0 us
  local copies, waits for them, and re-layouts: 36.4 us -> 12.5 us
  starting transfers between devices: 5.1 us -> 0 us
    pallas_call x0 -> x1, Pallas kernels: none -> 48.6 us  [per_device(): pl.pallas_call(functools.partial(kernel, n_ao, n_pb, chunks), out_shape=j...]
    dot_general x36 -> x0, matrix products: 40 us -> none  [the longest x8 18.3 us: per_device(): lax.dot_general(slot_data[c], chosen, (((1,), (1,)), ((), ())), preferred...]
    ppermute x2 -> x0, waiting for transfers between devices: 34.6 us -> none  [the longest x1 17.9 us: with_halo(): lax.ppermute(lax.slice_in_dim(block, 0, width, axis=dim), axis, backward)]
    reduce_scatter x1 -> x0, waiting for transfers between devices: 29.9 us -> none  [per_device(): lax.psum_scatter(partial_chi, ('ao', 'rep'), scatter_dimension=1, tiled=T...]
    reshape x11 -> x2, local copies, waits for them, and re-layouts: 12.6 us -> 2.21 us  [per_device(): g_occ[0].reshape(3, 32, 2, 32, 2).transpose(4, 2, 1, 0, 3).reshape(128, 96)]
    another operation x21 -> x1, local copies, waits for them, and re-layouts: 12.3 us -> 4.21 us  [per_device(): g_occ[0].reshape(3, 32, 2, 32, 2).transpose(4, 2, 1, 0, 3).reshape(128, 96)]
    slice x8 -> x0, local copies, waits for them, and re-layouts: 6.67 us -> none  [the longest x3 3.99 us: per_device(): extended_rows[d, s, :q_rows].reshape(q_rows * block_size, block_size)]
    ppermute x2 -> x0, starting transfers between devices: 5.05 us -> none  [the longest x1 5.05 us: with_halo(): lax.ppermute(lax.slice_in_dim(block, 0, width, axis=dim), axis, backward)]
  transfers between devices with their start and end apart: 4 -> 0, of which waited for: 3 -> 0; matrix products, arithmetic and copies ran while one was open for 5% -> 0% of each run, Pallas kernels for 0% -> 0%
where the time goes in v1:
time: 65.5 us; the launch traced here: 65.1 us
  Pallas kernels  48.6 us (74%)
  local copies, waits for them, and re-layouts  12.5 us (19%)
  blocking collectives  1.92 us (3%)
  other arithmetic  1.39 us (2%)
  between operations  0.71 us (1%)
    pallas_call x1, Pallas kernels, per_device(): pl.pallas_call(functools.partial(kernel, n_ao, n_pb, chunks), out_shape=j...  48.6 us
    unnamed x10, local copies, waits for them, and re-layouts  4.66 us
    another operation x1, local copies, waits for them, and re-layouts, per_device(): g_occ[0].reshape(3, 32, 2, 32, 2).transpose(4, 2, 1, 0, 3).reshape(128, 96)  4.21 us
    reshape x2, local copies, waits for them, and re-layouts, per_device(): g_occ[0].reshape(3, 32, 2, 32, 2).transpose(4, 2, 1, 0, 3).reshape(128, 96)  2.21 us
    unnamed x1, blocking collectives  1.92 us

profile of v1, /device:TPU:0, one launch (start us, length us, event | category | flops | bytes accessed | tf_op | source)
XLA Modules:
  0.0 65.1 jit_solution(3906862601670095281)
XLA Ops:
  0.0 0.0 copy-start
  0.0 0.0 copy-start.1
  0.0 1.1 %copy-done = bf16[1,3,32,4096]{3,2,1,0:T(8,128)(2,1)S(1)} copy-done((bf16[1,3,32,4096]{3,2,1,0:T(8,128)(2,1)S(1)}, bf16[1,3,32,4096]{3,2,1,0:T(8,128)(2,1)}, u32[]{:S(2)}) %copy-start) | copy-done | bytes 786456
  1.2 0.1 copy.19
  1.2 0.8 %copy_bitcast_fusion.tq = bf16[16,3,32,128]{3,2,1,0:T(8,128)(2,1)} fusion(bf16[3,16,32,128]{3,2,1,0:T(8,128)(2,1)S(1)} %bitcast.24), kind=kLoop, calls=%fused_computation | loop fusion | bytes 786432 | tf_op jit(solution)/shard_map/transpose | solution.py:213
  2.0 1.2 %dynamic-slice.1 = u32[1]{0:T(128)} dynamic-slice(u32[32]{0:T(128)} %constant.26, u32[]{:T(128)S(6)} %add.6), dynamic_slice_sizes={1} | dynamic-slice | bytes 12
  3.9 0.8 %bitcast_dynamic-update-slice_fusion = s32[16]{0:T(128)S(1)} fusion(s32[16]{0:T(128)S(1)} %broadcast.3, u32[]{:T(128)} %bitcast.1, s32[1,8]{1,0:T(1,128)} %param.9), kind=kLoop, calls=%fused_computation.4 | loop fusion | bytes 100
  4.7 1.9 %all-reduce.1 = s32[16]{0:T(128)S(1)} all-reduce(s32[16]{0:T(128)S(1)} %bitcast_dynamic-update-slice_fusion), channel_id=2, replica_groups=mesh['grp'=2,'ao'=4,'pb'=2,'rep'=2] {'rep'}, use_global_device_ids=true, to_apply=%add.1 | all-reduce | flops 16 | bytes 128
  6.6 0.7 %select_reduce_fusion.inv = s32[24]{0:T(128)} fusion(s32[16]{0:T(128)S(1)} %all-reduce.1), kind=kLoop, calls=%fused_computation.2 | loop fusion | flops 1128 | bytes 160 | tf_op jit(solution)/shard_map/reduce_min | solution.py:222
  7.3 4.2 %reshape_squeeze.3 = bf16[3,32,2,32,2]{4,3,2,1,0:T(8,128)(2,1)S(1)} reshape(bf16[1,3,64,64]{3,2,1,0:T(8,128)(2,1)} %param.5) | data formatting | bytes 49152 | tf_op jit(solution)/shard_map/reshape;squeeze | solution.py:216
  11.5 2.1 %copy.17 = bf16[2,2,32,3,32]{4,3,2,1,0:T(4,128)(2,1)S(1)} copy(bf16[2,2,32,3,32]{0,4,1,2,3:T(8,128)(2,1)S(1)} %bitcast.22) | data formatting | bytes 49152 | tf_op jit(solution)/shard_map/reshape | solution.py:216
  13.6 0.1 reshape.18
  13.7 0.6 pad.4.go_in
  14.3 0.0 copy-done.1
  14.3 0.1 copy.14
  14.4 0.7 %pad_maximum_fusion.gv_in = bf16[3,64,128]{2,1,0:T(8,128)(2,1)} fusion(bf16[3,64,64]{2,1,0:T(8,128)(2,1)S(1)} %bitcast.26), kind=kLoop, calls=%fused_computation.1 | loop fusion | flops 98304 | bytes 73728 | tf_op jit(solution)/shard_map/concatenate | solution.py:215
  15.1 48.6 %shard_map.55 = f32[16,512]{1,0:T(8,128)} custom-call(s32[24]{0:T(128)} %select_reduce_fusion.inv, bf16[16,3,32,128]{3,2,1,0:T(8,128)(2,1)} %copy_bitcast_fusion.tq, bf16[3,64,128]{2,1,0:T(8,128)(2,1)} %pad_maximum_fusion.gv_in, bf16[128,128]{1,0:T(8,128)(2,1)} %pad.4.go_in, bf16[8,64,4096]{2,1,0:T(8,128)(2,1)} %bitcast.23), custom_call_target="tpu_custom_call" | custom-call | tf_op jit(solution)/shard_map/pallas_call | solution.py:228
  63.8 1.4 %copy.23 = f32[512,16]{0,1:T(8,128)} copy(f32[512,16]{0,1:T(8,128)} %bitcast.27) | data formatting | bytes 65536
  (2 shorter events, 0.0 us)
Async XLA Ops:
  0.0 1.1 %copy-start = (bf16[1,3,32,4096]{3,2,1,0:T(8,128)(2,1)S(1)}, bf16[1,3,32,4096]{3,2,1,0:T(8,128)(2,1)}, u32[]{:S(2)}) copy-start(bf16[1,3,32,4096]{3,2,1,0:T(8,128)(2,1)} %param.7) | copy-start | bytes 2359300
  0.0 14.3 %copy-start.1 = (bf16[1,3,64,64]{3,2,1,0:T(8,128)(2,1)S(1)}, bf16[1,3,64,64]{3,2,1,0:T(8,128)(2,1)}, u32[]{:S(2)}) copy-start(bf16[1,3,64,64]{3,2,1,0:T(8,128)(2,1)} %param.6) | copy-start | bytes 73732

commit v2 on v1

--- a/solution.py
+++ b/solution.py
@@ -14,9 +14,9 @@
 PASS_CHUNKS = 2
 
 
-def kernel(n_ao, n_pb, chunks, inv, tq, gv_in, go_in, p_in, out,
-           tlo, thi, gv, go, bmat, glu, pbuf, xs, wsend, wbuf, wf, wt, chi, rs,
-           s_t, r_tlo, r_thi, s_gv, r_gv, s_go, r_go, s_p, r_p, l_sem,
+def kernel(n_ao, n_pb, chunks, codes, codes_v, tq_in, gv_in, go_in, p_in, out,
+           theirs_v, theirs_s, traw, turned, tq, tlo, thi, gv, go, bmat, glu, pbuf, xs, wsend, wbuf, wf, wt, chi, rs,
+           s_t, r_tlo, r_thi, s_gv, r_gv, s_go, r_go, s_p, r_p, s_id, r_id, l_sem,
            s_w, r_w, s_rs, r_rs):
     g, a = lax.axis_index("grp"), lax.axis_index("ao")
     p, r = lax.axis_index("pb"), lax.axis_index("rep")
@@ -28,6 +28,15 @@
 
     def from_p(step):
         return lax.rem(p + n_pb - step, n_pb)
+
+    q_half = traw.shape[1]
+    own_t = pltpu.make_async_copy(
+        tq_in.at[0, :, pl.ds(pl.multiple_of(g * q_half, q_half), q_half), :], traw, l_sem.at[1])
+    own_t.start()
+    half = p_in.shape[1]
+    mine = pl.ds(r * half, half)
+    own_p = pltpu.make_async_copy(p_in.at[0], pbuf.at[mine], l_sem.at[0])
+    own_p.start()
 
     barrier = pltpu.get_barrier_semaphore()
     peers = [(g, lax.rem(a + i, n_ao), p, j) for i in range(1, n_ao) for j in (0, 1)]
@@ -50,7 +59,7 @@
         copy.start()
         sends.append(copy)
 
-    post(go_in, go.at[1], s_go.at[0], r_go.at[0], (other, a, p, r))
+    post(go_in, go, s_go.at[0], r_go.at[0], (other, a, p, r))
     count = 0
     for dg, grp in ((0, g), (1, other)):
         for n, row in ((0, up), (1, a), (2, down)):
@@ -58,44 +67,66 @@
                 continue
             post(gv_in, gv.at[dg, n], s_gv.at[count], r_gv.at[dg * 3 + n], (grp, row, p, r))
             count += 1
+    post(codes_v, theirs_v, s_id.at[0], r_id.at[0], (g, a, p, 1 - r))
+    post(p_in.at[0], pbuf.at[mine], s_p.at[0], r_p.at[0], (g, a, p, 1 - r))
+
+    own_t.wait()
+    for s in range(3):
+        for tile in range(32):
+            turned[s, tile * q_half:(tile + 1) * q_half] = (
+                traw[s, :, tile * 128:(tile + 1) * 128].astype(F32))
     for c in range(chunks):
+        for q in range(c * CHUNK_Q, (c + 1) * CHUNK_Q):
+            for s in range(3):
+                tq[q, s] = turned[s, pl.ds(q, 32, stride=q_half), :].astype(BF)
         rows = pl.ds(c * CHUNK_Q, CHUNK_Q)
         post(tq.at[rows], tlo.at[rows], s_t.at[2 * c], r_tlo.at[c], (g, up, p, r))
         post(tq.at[rows], thi.at[rows], s_t.at[2 * c + 1], r_thi.at[c], (g, down, p, r))
-    half = p_in.shape[0]
-    mine = pl.ds(r * half, half)
-    post(p_in, pbuf.at[mine], s_p.at[0], r_p.at[0], (g, a, p, 1 - r))
-    own_p = pltpu.make_async_copy(p_in, pbuf.at[mine], l_sem.at[0])
-    own_p.start()
     pbuf[2 * half] = jnp.zeros(pbuf.shape[1:], BF)
 
     def landed(dst, sem):
         remote(dst, dst, s_go.at[0], sem, (other, a, p, r)).wait_recv()
 
-    go[0] = go_in[...]
-    gv[0, 1] = gv_in[...]
-    landed(go.at[1], r_go.at[0])
-    lane = lax.broadcasted_iota(jnp.int32, (128, 128), 1)
+    def spread(low):
+        k = lax.broadcasted_iota(jnp.int32, (64, 128), 0)
+        to = lax.broadcasted_iota(jnp.int32, (64, 128), 1) - low
+        inside = (to >= 0) & (to < 32)
+        return [jnp.where(inside & (k == 2 * to + kl), 1.0, 0.0).astype(BF) for kl in range(2)]
+
+    row = lax.broadcasted_iota(jnp.int32, (64, 64), 0)
+    col = lax.broadcasted_iota(jnp.int32, (64, 64), 1)
+    order = jnp.where(col == 2 * lax.rem(row, 32) + row // 32, 1.0, 0.0).astype(BF)
+    lane = lax.broadcasted_iota(jnp.int32, (64, 128), 1)
+    spreads = [spread(32 * d) for d in range(3)]
     for dg in range(2):
-        whole = go[dg]
-        for u in range(5):
-            low, high = 32 * max(0, u - 2), 32 * (min(2, u) + 1)
-            glu[u, dg * 128:(dg + 1) * 128, :] = jnp.where(
-                (lane >= low) & (lane < high), whole, jnp.zeros_like(whole))
-    lane = lax.broadcasted_iota(jnp.int32, (64, 128), 1)
+        if dg == 1:
+            landed(go, r_go.at[0])
+        from_g = go_in.at[0] if dg == 0 else go.at[0]
+        sorted_rows = [jnp.dot(order, from_g[d], preferred_element_type=F32).astype(BF)
+                       for d in range(3)]
+        for kl in range(2):
+            terms = [jnp.dot(sorted_rows[d], spreads[d][kl], preferred_element_type=F32)
+                     for d in range(3)]
+            whole = terms[0] + terms[1] + terms[2]
+            at = dg * 128 + kl * 64
+            for u in range(5):
+                low, high = 32 * max(0, u - 2), 32 * (min(2, u) + 1)
+                glu[u, at:at + 64, :] = jnp.where(
+                    (lane >= low) & (lane < high), whole, jnp.zeros_like(whole)).astype(BF)
     for dg in range(2):
         for n in range(3):
-            if not (dg == 0 and n == 1):
+            own = dg == 0 and n == 1
+            if not own:
                 landed(gv.at[dg, n], r_gv.at[dg * 3 + n])
+            from_g = gv_in.at[0] if own else gv.at[dg, n, 0]
             for t in range(3):
-                both = gv[dg, n, t]
-                left = jnp.where(lane < 64, both, jnp.zeros_like(both))
-                right = jnp.where(lane < 64, jnp.zeros_like(both), both)
+                one = from_g[t]
+                both = jnp.concatenate((one, one), axis=1)
                 k = (dg * 3 + n) * 3 + t
-                bmat[k, 0:64] = left
-                bmat[k, 64:128] = left
-                bmat[k, 128:192] = right
-                bmat[k, 192:256] = right
+                bmat[k, 0:64, 0:128] = both
+                bmat[k, 0:64, 128:256] = jnp.zeros_like(both)
+                bmat[k, 64:128, 0:128] = jnp.zeros_like(both)
+                bmat[k, 64:128, 128:256] = both
 
     pair_lane = lax.rem(lax.broadcasted_iota(jnp.int32, (64, 256), 1), 128) < 64
     sources = [(dg, dp) for dg in range(2) for dp in range(n_pb)]
@@ -126,8 +157,9 @@
             for n in range(3):
                 total = jnp.zeros((rows_w, 128), F32)
                 for t in range(3):
-                    total = total + jnp.dot(
-                        xs[dg, n + t], bmat[(dg * 3 + n) * 3 + t], preferred_element_type=F32)
+                    total = total + lax.dot_general(
+                        xs[dg, n + t], bmat[(dg * 3 + n) * 3 + t], (((1,), (1,)), ((), ())),
+                        preferred_element_type=F32)
                 wsend[c, dg, n] = total.astype(BF)
             grp = g if dg == 0 else other
             for dp in range(n_pb):
@@ -136,6 +168,13 @@
                 k = c * len(sources) + dg * n_pb + dp
                 post(wsend.at[c, dg], wbuf.at[c, dg * n_pb + dp], s_w.at[k], r_w.at[k],
                      (grp, a, at_p(dp), r))
+
+    def slot_of(code):
+        slot = jnp.int32(2 * half)
+        for i in range(half):
+            slot = jnp.where(codes[0, i] == code, r * half + i, slot)
+            slot = jnp.where(theirs_s[0, i] == code, (1 - r) * half + i, slot)
+        return slot
 
     def contract(first):
         for c in range(first, first + PASS_CHUNKS):
@@ -156,7 +195,7 @@
             for n in range(3):
                 blocks = []
                 for i in range(4):
-                    blocks.append(pbuf[inv[(group * 4 + i) * 3 + n]])
+                    blocks.append(pbuf[slots[(group * 4 + i) * 3 + n]])
                 total = total + lax.dot_general(
                     wt[n], jnp.concatenate(blocks, axis=0), (((1,), (1,)), ((), ())),
                     preferred_element_type=F32)
@@ -167,12 +206,15 @@
 
     for c in range(chunks):
         make_w(c)
-        if c == PASS_CHUNKS:
-            own_p.wait()
-            theirs = pl.ds((1 - r) * half, half)
-            landed(pbuf.at[theirs], r_p.at[0])
-            contract(0)
-    contract(PASS_CHUNKS)
+    landed(theirs_v, r_id.at[0])
+    ids = pltpu.make_async_copy(theirs_v, theirs_s, l_sem.at[2])
+    ids.start()
+    ids.wait()
+    slots = [slot_of(code) for code in range(24)]
+    own_p.wait()
+    landed(pbuf.at[pl.ds((1 - r) * half, half)], r_p.at[0])
+    for first in range(0, chunks, PASS_CHUNKS):
+        contract(first)
 
     later = []
     for k, (dg, dp) in enumerate(sources):
@@ -208,19 +250,7 @@
 def per_device(n_ao, n_pb, g_occ, g_vir, three_q, three_centre_p, slot_ids):
     q_half = three_q.shape[2] // 2
     chunks = q_half // CHUNK_Q
-    g = lax.axis_index("grp")
-    tq = lax.dynamic_slice_in_dim(three_q[0], g * q_half, q_half, axis=1)
-    tq = tq.reshape(3, q_half, 32, 128).transpose(1, 0, 2, 3)
-    gv = g_vir[0].transpose(0, 2, 1)
-    gv = jnp.concatenate((gv, gv), axis=2)
-    go = g_occ[0].reshape(3, 32, 2, 32, 2).transpose(4, 2, 1, 0, 3).reshape(128, 96)
-    go = jnp.pad(go, ((0, 0), (0, 32)))
     slots = slot_ids.shape[1]
-    codes = lax.all_gather(slot_ids[0], "rep", tiled=True)
-    hit = codes[None, :] == jnp.arange(3 * slots, dtype=jnp.int32)[:, None]
-    numbers = jnp.arange(2 * slots, dtype=jnp.int32)
-    inv = jnp.min(jnp.where(hit, numbers[None, :], 2 * slots), axis=1)
-    p_flat = three_centre_p[0]
     n_src = 2 * n_pb
     count_q = n_src * PASS_CHUNKS * CHUNK_Q
     dma = pltpu.SemaphoreType.DMA
@@ -228,15 +258,21 @@
     out = pl.pallas_call(
         functools.partial(kernel, n_ao, n_pb, chunks),
         out_shape=jax.ShapeDtypeStruct((q_half, slots * 64), F32),
-        in_specs=[pl.BlockSpec(memory_space=pltpu.SMEM), vmem, vmem, vmem,
+        in_specs=[pl.BlockSpec(memory_space=pltpu.SMEM), vmem,
+                  pl.BlockSpec(memory_space=pl.ANY), vmem, vmem,
                   pl.BlockSpec(memory_space=pl.ANY)],
         out_specs=vmem,
         scratch_shapes=[
+            pltpu.VMEM((1, slots), jnp.int32),
+            pltpu.SMEM((1, slots), jnp.int32),
+            pltpu.VMEM((3, q_half, 4096), BF),
+            pltpu.VMEM((3, 32 * q_half, 128), F32),
             pltpu.VMEM((q_half, 3, 32, 128), BF),
             pltpu.VMEM((q_half, 3, 32, 128), BF),
-            pltpu.VMEM((2, 3, 3, 64, 128), BF),
-            pltpu.VMEM((2, 128, 128), BF),
-            pltpu.VMEM((18, 256, 128), BF),
+            pltpu.VMEM((q_half, 3, 32, 128), BF),
+            pltpu.VMEM((2, 3, 1, 3, 64, 64), BF),
+            pltpu.VMEM((1, 3, 64, 64), BF),
+            pltpu.VMEM((18, 128, 256), BF),
             pltpu.VMEM((5, 256, 128), BF),
             pltpu.VMEM((2 * slots + 1, 64, 4096), BF),
             pltpu.VMEM((2, 5, CHUNK_Q * 32, 256), BF),
@@ -247,13 +283,14 @@
             pltpu.VMEM((n_src, q_half, slots * 64), F32),
             pltpu.VMEM((n_ao, q_half, slots * 64), F32),
             dma((2 * chunks,)), dma((chunks,)), dma((chunks,)),
-            dma((5,)), dma((6,)), dma((1,)), dma((1,)), dma((1,)), dma((1,)), dma((1,)),
+            dma((5,)), dma((6,)), dma((1,)), dma((1,)), dma((1,)), dma((1,)),
+            dma((1,)), dma((1,)), dma((3,)),
             dma((chunks * n_src,)), dma((chunks * n_src,)),
             dma((n_src,)), dma((n_ao,)),
         ],
         compiler_params=pltpu.CompilerParams(
             collective_id=0, has_side_effects=True, vmem_limit_bytes=56 * 1024 * 1024),
-    )(inv, tq, gv, go, p_flat)
+    )(slot_ids, slot_ids, three_q, g_vir, g_occ, three_centre_p)
     return out.T
 
 

time: 65.5 us -> 48.4 us (0.74)
  local copies, waits for them, and re-layouts: 12.5 us -> 1.38 us
  blocking collectives: 1.92 us -> 0 us
  Pallas kernels: 48.6 us -> 46.7 us
  other arithmetic: 1.39 us -> 0 us
  between operations: 0.71 us -> 0.01 us
    another operation x1 -> x0, local copies, waits for them, and re-layouts: 4.21 us -> none  [per_device(): g_occ[0].reshape(3, 32, 2, 32, 2).transpose(4, 2, 1, 0, 3).reshape(128, 96)]
    unnamed x10 -> x1, local copies, waits for them, and re-layouts: 4.66 us -> 1.38 us
    reshape x2 -> x0, local copies, waits for them, and re-layouts: 2.21 us -> none  [per_device(): g_occ[0].reshape(3, 32, 2, 32, 2).transpose(4, 2, 1, 0, 3).reshape(128, 96)]
    unnamed x1 -> x0, blocking collectives: 1.92 us -> none
    pallas_call x1, Pallas kernels: 48.6 us -> 46.7 us  [per_device(): pl.pallas_call(functools.partial(kernel, n_ao, n_pb, chunks), out_shape=j...]
    transpose x1 -> x0, local copies, waits for them, and re-layouts: 0.76 us -> none  [per_device(): tq = tq.reshape(3, q_half, 32, 128).transpose(1, 0, 2, 3)]
    concatenate x1 -> x0, other arithmetic: 0.71 us -> none  [per_device(): gv = jnp.concatenate((gv, gv), axis=2)]
    reduce_min x1 -> x0, other arithmetic: 0.68 us -> none  [per_device(): inv = jnp.min(jnp.where(hit, numbers[None, :], 2 * slots), axis=1)]
where the time goes in v2:
time: 48.4 us; the launch traced here: 48.1 us
  Pallas kernels  46.7 us (96%)
  local copies, waits for them, and re-layouts  1.38 us (3%)
    pallas_call x1, Pallas kernels, per_device(): pl.pallas_call(functools.partial(kernel, n_ao, n_pb, chunks), out_shape=j...  46.7 us
    unnamed x1, local copies, waits for them, and re-layouts  1.38 us

profile of v2, /device:TPU:0, one launch (start us, length us, event | category | flops | bytes accessed | tf_op | source)
XLA Modules:
  0.0 48.1 jit_solution(7718173606406294389)
XLA Ops:
  0.0 46.7 %shard_map.55 = f32[16,512]{1,0:T(8,128)} custom-call(s32[1,8]{1,0:T(1,128)} %codes_v.1, s32[1,8]{1,0:T(1,128)} %codes_v.1, bf16[1,3,32,4096]{3,2,1,0:T(8,128)(2,1)} %tq_in.1, bf16[1,3,64,64]{3,2,1,0:T(8,128)(2,1)} %gv_in.1, bf16[1,3,64,64]{3,2,1,0:T(8,128)(2,1)} %go_in.1, bf16[1,8,64,4096]{3,2,1,0:T(8,128)(2,1)} %p_in.1), custom_call_target="tpu_custom_call" | custom-call | tf_op jit(solution)/shard_map/pallas_call | solution.py:258
  46.7 1.4 %copy.7 = f32[512,16]{0,1:T(8,128)} copy(f32[512,16]{0,1:T(8,128)} %bitcast.1) | data formatting | bytes 65536

commit v3 on v2

--- a/solution.py
+++ b/solution.py
@@ -11,11 +11,10 @@
 BF = jnp.bfloat16
 F32 = jnp.float32
 CHUNK_Q = 4
-PASS_CHUNKS = 2
 
 
 def kernel(n_ao, n_pb, chunks, codes, codes_v, tq_in, gv_in, go_in, p_in, out,
-           theirs_v, theirs_s, traw, turned, tq, tlo, thi, gv, go, bmat, glu, pbuf, xs, wsend, wbuf, wf, wt, chi, rs,
+           theirs_v, theirs_s, prod, traw, turned, tq, tlo, thi, gv, go, bmat, glu, pbuf, xs, wsend, wbuf, wf, wt, chi, rs,
            s_t, r_tlo, r_thi, s_gv, r_gv, s_go, r_go, s_p, r_p, s_id, r_id, l_sem,
            s_w, r_w, s_rs, r_rs):
     g, a = lax.axis_index("grp"), lax.axis_index("ao")
@@ -82,7 +81,6 @@
         rows = pl.ds(c * CHUNK_Q, CHUNK_Q)
         post(tq.at[rows], tlo.at[rows], s_t.at[2 * c], r_tlo.at[c], (g, up, p, r))
         post(tq.at[rows], thi.at[rows], s_t.at[2 * c + 1], r_thi.at[c], (g, down, p, r))
-    pbuf[2 * half] = jnp.zeros(pbuf.shape[1:], BF)
 
     def landed(dst, sem):
         remote(dst, dst, s_go.at[0], sem, (other, a, p, r)).wait_recv()
@@ -176,36 +174,53 @@
             slot = jnp.where(theirs_s[0, i] == code, (1 - r) * half + i, slot)
         return slot
 
-    def contract(first):
-        for c in range(first, first + PASS_CHUNKS):
-            for k in range(len(sources)):
-                if k > 0:
-                    landed(wbuf.at[c, k], r_w.at[c * len(sources) + k])
-                for n in range(3):
-                    block = wsend[c, 0, n] if k == 0 else wbuf[c, k, n]
-                    at = (k * PASS_CHUNKS + c - first) * rows_w
-                    wf[n, at:at + rows_w] = block.astype(F32)
-        count_q = len(sources) * PASS_CHUNKS * CHUNK_Q
+    n_src = len(sources)
+    chunk_rows = n_src * CHUNK_Q
+
+    def gather(c):
+        for k in range(n_src):
+            if k > 0:
+                landed(wbuf.at[c, k], r_w.at[c * n_src + k])
+            for n in range(3):
+                block = wsend[c, 0, n] if k == 0 else wbuf[c, k, n]
+                wf[n, k * rows_w:(k + 1) * rows_w] = block.astype(F32)
         for n in range(3):
+            at = n * chunks * chunk_rows + c * chunk_rows
             for tile in range(32):
-                wt[n, :, tile * 128:(tile + 1) * 128] = wf[
-                    n, pl.ds(tile, count_q, stride=32), :].astype(BF)
-        for group in range(2):
-            total = jnp.zeros((count_q, 256), F32)
+                wt[at:at + chunk_rows, tile * 128:(tile + 1) * 128] = wf[
+                    n, pl.ds(tile, chunk_rows, stride=32), :].astype(BF)
+
+    def contract():
+        count_q = chunks * chunk_rows
+        low = lax.broadcasted_iota(jnp.int32, (count_q, 128), 1) < 64
+        for n in range(3):
+            prod[n, 2 * half] = jnp.zeros((count_q, 128), F32)
+        for four in range(0, 2 * half, 4):
+            both = jnp.concatenate([pbuf[four + i] for i in range(4)], axis=0)
+            total = lax.dot_general(
+                wt[...], both, (((1,), (1,)), ((), ())), preferred_element_type=F32)
             for n in range(3):
-                blocks = []
-                for i in range(4):
-                    blocks.append(pbuf[slots[(group * 4 + i) * 3 + n]])
-                total = total + lax.dot_general(
-                    wt[n], jnp.concatenate(blocks, axis=0), (((1,), (1,)), ((), ())),
-                    preferred_element_type=F32)
-            for k in range(len(sources)):
-                width = PASS_CHUNKS * CHUNK_Q
-                chi[k, first * CHUNK_Q:first * CHUNK_Q + width, group * 256:(group + 1) * 256] = (
-                    total[k * width:(k + 1) * width])
+                for i in range(2):
+                    tile = total[n * count_q:(n + 1) * count_q, i * 128:(i + 1) * 128]
+                    turn = pltpu.roll(tile, 64, 1)
+                    prod[n, four + 2 * i] = jnp.where(low, tile, turn)
+                    prod[n, four + 2 * i + 1] = jnp.where(low, turn, tile)
+        for pair in range(half // 2):
+            sides = []
+            for block in (2 * pair, 2 * pair + 1):
+                at = [slots[block * 3 + n] for n in range(3)]
+                sides.append(prod[0, at[0]] + prod[1, at[1]] + prod[2, at[2]])
+            total = jnp.where(low, sides[0], sides[1])
+            for c in range(chunks):
+                for k in range(n_src):
+                    at = c * chunk_rows + k * CHUNK_Q
+                    chi[k, c * CHUNK_Q:(c + 1) * CHUNK_Q, pair * 128:(pair + 1) * 128] = (
+                        total[at:at + CHUNK_Q])
 
     for c in range(chunks):
         make_w(c)
+        if c >= 2:
+            gather(c - 2)
     landed(theirs_v, r_id.at[0])
     ids = pltpu.make_async_copy(theirs_v, theirs_s, l_sem.at[2])
     ids.start()
@@ -213,8 +228,9 @@
     slots = [slot_of(code) for code in range(24)]
     own_p.wait()
     landed(pbuf.at[pl.ds((1 - r) * half, half)], r_p.at[0])
-    for first in range(0, chunks, PASS_CHUNKS):
-        contract(first)
+    for c in range(chunks - 2, chunks):
+        gather(c)
+    contract()
 
     later = []
     for k, (dg, dp) in enumerate(sources):
@@ -252,7 +268,7 @@
     chunks = q_half // CHUNK_Q
     slots = slot_ids.shape[1]
     n_src = 2 * n_pb
-    count_q = n_src * PASS_CHUNKS * CHUNK_Q
+    count_q = n_src * CHUNK_Q
     dma = pltpu.SemaphoreType.DMA
     vmem = pl.BlockSpec(memory_space=pltpu.VMEM)
     out = pl.pallas_call(
@@ -265,6 +281,7 @@
         scratch_shapes=[
             pltpu.VMEM((1, slots), jnp.int32),
             pltpu.SMEM((1, slots), jnp.int32),
+            pltpu.VMEM((3, 2 * slots + 1, chunks * count_q, 128), F32),
             pltpu.VMEM((3, q_half, 4096), BF),
             pltpu.VMEM((3, 32 * q_half, 128), F32),
             pltpu.VMEM((q_half, 3, 32, 128), BF),
@@ -274,12 +291,12 @@
             pltpu.VMEM((1, 3, 64, 64), BF),
             pltpu.VMEM((18, 128, 256), BF),
             pltpu.VMEM((5, 256, 128), BF),
-            pltpu.VMEM((2 * slots + 1, 64, 4096), BF),
+            pltpu.VMEM((2 * slots, 64, 4096), BF),
             pltpu.VMEM((2, 5, CHUNK_Q * 32, 256), BF),
             pltpu.VMEM((chunks, 2, 3, CHUNK_Q * 32, 128), BF),
             pltpu.VMEM((chunks, n_src, 3, CHUNK_Q * 32, 128), BF),
             pltpu.VMEM((3, count_q * 32, 128), F32),
-            pltpu.VMEM((3, count_q, 4096), BF),
+            pltpu.VMEM((3 * chunks * count_q, 4096), BF),
             pltpu.VMEM((n_src, q_half, slots * 64), F32),
             pltpu.VMEM((n_ao, q_half, slots * 64), F32),
             dma((2 * chunks,)), dma((chunks,)), dma((chunks,)),

time: 48.4 us -> 47.4 us (0.979)
  Pallas kernels: 46.7 us -> 45.8 us
    pallas_call x1, Pallas kernels: 46.7 us -> 45.8 us  [per_device(): pl.pallas_call(functools.partial(kernel, n_ao, n_pb, chunks), out_shape=j...]
where the time goes in v3:
time: 47.4 us; the launch traced here: 47.1 us
  Pallas kernels  45.8 us (97%)
  local copies, waits for them, and re-layouts  1.38 us (3%)
    pallas_call x1, Pallas kernels, per_device(): pl.pallas_call(functools.partial(kernel, n_ao, n_pb, chunks), out_shape=j...  45.8 us
    unnamed x1, local copies, waits for them, and re-layouts  1.38 us

profile of v3, /device:TPU:0, one launch (start us, length us, event | category | flops | bytes accessed | tf_op | source)
XLA Modules:
  0.0 47.1 jit_solution(8526524123023665918)
XLA Ops:
  0.0 45.8 %shard_map.55 = f32[16,512]{1,0:T(8,128)} custom-call(s32[1,8]{1,0:T(1,128)} %codes_v.1, s32[1,8]{1,0:T(1,128)} %codes_v.1, bf16[1,3,32,4096]{3,2,1,0:T(8,128)(2,1)} %tq_in.1, bf16[1,3,64,64]{3,2,1,0:T(8,128)(2,1)} %gv_in.1, bf16[1,3,64,64]{3,2,1,0:T(8,128)(2,1)} %go_in.1, bf16[1,8,64,4096]{3,2,1,0:T(8,128)(2,1)} %p_in.1), custom_call_target="tpu_custom_call" | custom-call | tf_op jit(solution)/shard_map/pallas_call | solution.py:274
  45.8 1.4 %copy.7 = f32[512,16]{0,1:T(8,128)} copy(f32[512,16]{0,1:T(8,128)} %bitcast.1) | data formatting | bytes 65536

commit v4 on v3

--- a/solution.py
+++ b/solution.py
@@ -198,7 +198,7 @@
         for four in range(0, 2 * half, 4):
             both = jnp.concatenate([pbuf[four + i] for i in range(4)], axis=0)
             total = lax.dot_general(
-                wt[...], both, (((1,), (1,)), ((), ())), preferred_element_type=F32)
+                both, wt[...], (((1,), (1,)), ((), ())), preferred_element_type=F32).T
             for n in range(3):
                 for i in range(2):
                     tile = total[n * count_q:(n + 1) * count_q, i * 128:(i + 1) * 128]

time: 47.4 us -> 47 us (level)
  no operation moved by 1% of the time
where the time goes in v4:
time: 47 us; the launch traced here: 46.7 us
  Pallas kernels  45.4 us (97%)
  local copies, waits for them, and re-layouts  1.38 us (3%)
    pallas_call x1, Pallas kernels, per_device(): pl.pallas_call(functools.partial(kernel, n_ao, n_pb, chunks), out_shape=j...  45.4 us
    unnamed x1, local copies, waits for them, and re-layouts  1.38 us

profile of v4, /device:TPU:0, one launch (start us, length us, event | category | flops | bytes accessed | tf_op | source)
XLA Modules:
  0.0 46.7 jit_solution(2882430449714471544)
XLA Ops:
  0.0 45.4 %shard_map.55 = f32[16,512]{1,0:T(8,128)} custom-call(s32[1,8]{1,0:T(1,128)} %codes_v.1, s32[1,8]{1,0:T(1,128)} %codes_v.1, bf16[1,3,32,4096]{3,2,1,0:T(8,128)(2,1)} %tq_in.1, bf16[1,3,64,64]{3,2,1,0:T(8,128)(2,1)} %gv_in.1, bf16[1,3,64,64]{3,2,1,0:T(8,128)(2,1)} %go_in.1, bf16[1,8,64,4096]{3,2,1,0:T(8,128)(2,1)} %p_in.1), custom_call_target="tpu_custom_call" | custom-call | tf_op jit(solution)/shard_map/pallas_call | solution.py:274
  45.4 1.4 %copy.7 = f32[512,16]{0,1:T(8,128)} copy(f32[512,16]{0,1:T(8,128)} %bitcast.1) | data formatting | bytes 65536
